TPU v7x, 256 devices: a whole 4x4x8 slice. The times are simulated.
256 devices in a mesh: depth: 32 (over x, y, core), tile: 8 (over z).
Axes of the slice: x: 4, y: 4, z: 8, core: 2. Of those that a mesh axis runs over, the one named last changes fastest.
Arguments:
- fronts: float32 [32, 8, 8, 2, 128, 128], P('depth', 'tile'), may hold values from -6 to 6
- probe_wave: float32 [2, 128, 128], replicated, may hold values from -6 to 6
- object_slices: bfloat16 [64, 2, 3072, 384], P('depth', None, 'tile')
- patch_list: int32 [35, 8, 3, 8], P(None, 'tile'), may hold values from 0 to 256, as said below
- counts: int32 [35, 8], P(None, 'tile'), may hold values from 1 to 8, as said below
Outputs:
- exit_waves: float32 [32, 8, 8, 2, 128, 128], P('depth', 'tile')
Inputs may be any that keep to these rules, and one draw needn't show every extreme that they name: `patch_list`: rows and columns of corners run from 0 to 256, and that end is reached. Among the live probes of one batch of one owner no tile is named more than 1 times; a batch of 8 probes names every tile exactly 1 times. `counts`: some batch of some owner holds 8 probes.
All inputs are finite; a program needn't handle non-finite values.
Results may differ from a plain program's by a relative error of at most 0.0003.
Values may be sent and summed in bfloat16 or wider, within the bound.
A program may use at most 64 MiB of HBM per device.

v0:
```python
import math

import jax
import jax.numpy as jnp
from jax import lax
from jax.sharding import PartitionSpec as P

STEPS = 4


fresnel_rate = 0.3


def from_behind(value, axis, steps):
    count = lax.axis_size(axis)
    leading, last = (max(0, -steps), min(count, count - steps))
    return lax.ppermute(value, axis, [(source, source + steps) for source in range(leading, last)])


def dft_tables(width, inverse):
    index = jnp.arange(width, dtype=jnp.int32)
    angle = 2.0 * math.pi / width * (index[:, None] * index[None, :] % width).astype(jnp.float32)
    cosine = jnp.cos(angle)
    sine = jnp.sin(angle)
    if inverse:
        cosine = cosine / width
        imagine = sine / width
    else:
        imagine = -sine
    return (cosine, cosine + imagine, imagine - cosine)


def plane_dot(plane, table):
    shape = plane.shape
    flat = plane.reshape(-1, shape[-1])
    return jnp.dot(
        flat, table, precision=lax.Precision.HIGHEST, preferred_element_type=jnp.float32
    ).reshape(shape)


def right_multiply(real_part, imag_part, tables):
    cosine, summed, differ = tables
    first = plane_dot(real_part + imag_part, cosine)
    second = plane_dot(real_part, differ)
    third = plane_dot(imag_part, summed)
    return (first - third, first + second)


def transform(real_part, imag_part, tables):
    real_part, imag_part = right_multiply(real_part, imag_part, tables)
    return right_multiply(jnp.swapaxes(real_part, -1, -2), jnp.swapaxes(imag_part, -1, -2), tables)


def fresnel(width):
    index = jnp.arange(width, dtype=jnp.int32)
    freq = jnp.where(index < width // 2, index, index - width).astype(jnp.float32)
    phase = -2.0 * math.pi * fresnel_rate / width * (freq[:, None] ** 2 + freq[None, :] ** 2)
    return (jnp.cos(phase), jnp.sin(phase))


def slab_pass(wavefield, patches):
    width = wavefield.shape[-1]
    forward = dft_tables(width, False)
    backward = dft_tables(width, True)
    kernel_cos, kernel_sin = fresnel(width)
    real_part = wavefield[:, 0]
    imag_part = wavefield[:, 1]
    for layer in range(2):
        trans_real = patches[:, layer, 0].astype(jnp.float32)
        trans_imag = patches[:, layer, 1].astype(jnp.float32)
        real_part, imag_part = (
            real_part * trans_real - imag_part * trans_imag,
            real_part * trans_imag + imag_part * trans_real,
        )
        spec_real, spec_imag = transform(real_part, imag_part, forward)
        spec_real, spec_imag = (
            spec_real * kernel_cos - spec_imag * kernel_sin,
            spec_real * kernel_sin + spec_imag * kernel_cos,
        )
        real_part, imag_part = transform(spec_real, spec_imag, backward)
    return jnp.stack([real_part, imag_part], axis=1)


def rank_within(tile_ids, live):
    slot_index = jnp.arange(tile_ids.shape[0], dtype=jnp.int32)
    same = (
        (tile_ids[:, None] == tile_ids[None, :])
        & live[None, :]
        & (slot_index[None, :] < slot_index[:, None])
    )
    return jnp.sum(same.astype(jnp.int32), axis=1)


def cut_from(source, row_value, column_value, width):
    zero = jnp.zeros((), jnp.int32)
    return lax.dynamic_slice(source, (zero, zero, row_value, column_value), (2, 2, width, width))


def per_device(fronts, probe_wave, object_slices, patch_list, counts):
    depth_count = lax.axis_size("depth")
    tile_count = lax.axis_size("tile")
    depth_index = lax.axis_index("depth")
    tile_index = lax.axis_index("tile")
    slots = fronts.shape[2]
    width = fronts.shape[-1]
    pair = slots // tile_count
    slot_index = jnp.arange(slots, dtype=jnp.int32)
    own_lists = patch_list[:, 0]
    own_counts = counts[:, 0]
    batch_ids = [step + depth_count - 1 - depth_index for step in range(STEPS)]
    step_lists = jnp.stack(
        [lax.dynamic_index_in_dim(own_lists, batch, 0, keepdims=False) for batch in batch_ids]
    )
    step_counts = jnp.stack(
        [lax.dynamic_index_in_dim(own_counts, batch, 0, keepdims=False) for batch in batch_ids]
    )

    def outgoing(all_lists, all_counts):
        tile_ids = all_lists[:, 0]
        live = slot_index[None, :] < all_counts[:, None]
        order = jax.vmap(rank_within)(tile_ids, live)
        target = live & (tile_ids == tile_index)
        choose = (
            target[:, None, :]
            & (order[:, None, :] == jnp.arange(pair, dtype=jnp.int32)[None, :, None])
        ).astype(jnp.int32)
        row_start = jnp.sum(choose * all_lists[:, 1][:, None, :], axis=-1)
        column_start = jnp.sum(choose * all_lists[:, 2][:, None, :], axis=-1)
        valid = jnp.sum(choose, axis=-1) > 0

        def cut_local(row_value, column_value):
            return cut_from(object_slices, row_value, column_value, width)

        cuts = jax.vmap(jax.vmap(cut_local))(row_start, column_start)
        return jnp.where(valid[:, :, None, None, None, None], cuts, jnp.zeros_like(cuts))

    wavefield = fronts[0, 0]
    for step in range(STEPS):
        listing = step_lists[step]
        count = step_counts[step]
        live = (slot_index < count).astype(jnp.float32)[:, None, None, None]
        if step > 0:
            arrived = from_behind(wavefield, "depth", 1)
            wavefield = jnp.where(depth_index == 0, probe_wave[None] * live, arrived)
        else:
            wavefield = wavefield * live
        got_lists, got_counts = (
            lax.all_gather(listing[None], "tile", axis=0, tiled=True),
            lax.all_gather(count[None], "tile", axis=0, tiled=True),
        )
        received = lax.all_to_all(
            outgoing(got_lists, got_counts), "tile", split_axis=0, concat_axis=0, tiled=True
        )
        incoming_tile_ids = listing[0]
        incoming_live = slot_index < count
        incoming_order = rank_within(incoming_tile_ids, incoming_live)
        place = incoming_tile_ids * pair + jnp.minimum(incoming_order, pair - 1)
        flat = received.reshape((tile_count * pair,) + received.shape[2:])
        patches = jnp.take(flat, place, axis=0)
        wavefield = slab_pass(wavefield, patches)
    return wavefield[None, None]


def solution(mesh):
    in_specs = (
        P("depth", "tile", None, None, None, None),
        P(),
        P("depth", None, "tile", None),
        P(None, "tile", None, None),
        P(None, "tile"),
    )
    out_specs = P("depth", "tile", None, None, None, None)
    return jax.shard_map(
        per_device, mesh=mesh, in_specs=in_specs, out_specs=out_specs, check_vma=False
    )
```

profile of v0, /device:TPU:6, one launch (start us, length us, event | category | flops | bytes accessed | tf_op | source)
XLA Modules:
  0.0 397.5 jit_solution(2629929279038056412)
XLA Ops:
  7.9 16.1 %all-reduce.4 = (s32[8]{0:T(128)S(1)}, s32[8]{0:T(128)S(1)}, s32[8]{0:T(128)S(1)}, s32[8]{0:T(128)S(1)}) all-reduce(s32[8]{0:T(128)S(1)} %bitcast_dynamic-update-slice_fusion.4, s32[8]{0:T(128)S(1)} %bitcast_dynamic-update-slice_fusion.5, s32[8]{0:T(128)S(1)} %bitcast_dynamic-update-slice_fusion.6, ...), channel_id=8, replica_groups=mesh['depth'=32,'tile'=8] {'tile'}, use_global_device_ids=true, to_apply=%add.3 | all-reduce | flops 32 | bytes 256 | tf_op jit(solution)/shard_map/all_gather | solution.py:149
  25.4 20.7 %all-gather.7 = s32[8,1,3,8]{3,1,2,0:T(1,128)S(1)} all-gather(s32[1,1,3,8]{3,1,2,0:T(1,128)S(1)} %copy.293), channel_id=9, replica_groups=mesh['depth'=32,'tile'=8] {'tile'}, dimensions={0}, use_global_device_ids=true | all-gather | bytes 864 | tf_op jit(solution)/shard_map/all_gather | solution.py:148
  46.2 21.4 %all-gather.5 = s32[8,1,3,8]{3,1,2,0:T(1,128)S(1)} all-gather(s32[1,1,3,8]{3,1,2,0:T(1,128)S(1)} %copy.292), channel_id=7, replica_groups=mesh['depth'=32,'tile'=8] {'tile'}, dimensions={0}, use_global_device_ids=true | all-gather | bytes 864 | tf_op jit(solution)/shard_map/all_gather | solution.py:148
  67.8 21.0 %all-gather.3 = s32[8,1,3,8]{3,1,2,0:T(1,128)S(1)} all-gather(s32[1,1,3,8]{3,1,2,0:T(1,128)S(1)} %copy.291), channel_id=5, replica_groups=mesh['depth'=32,'tile'=8] {'tile'}, dimensions={0}, use_global_device_ids=true | all-gather | bytes 864 | tf_op jit(solution)/shard_map/all_gather | solution.py:148
  88.9 21.2 %all-gather.1 = s32[8,1,3,8]{3,1,2,0:T(1,128)S(1)} all-gather(s32[1,1,3,8]{3,1,2,0:T(1,128)S(1)} %copy.290), channel_id=3, replica_groups=mesh['depth'=32,'tile'=8] {'tile'}, dimensions={0}, use_global_device_ids=true | all-gather | bytes 864 | tf_op jit(solution)/shard_map/all_gather | solution.py:148
  112.0 24.6 %while.4 = (s32[]{:T(128)}, bf16[2,2,384,384]{3,2,1,0:T(8,128)(2,1)}, s32[8,4]{0,1:T(4,128)S(1)}, bf16[8,2,2,128,128]{4,3,2,1,0:T(8,128)(2,1)S(1)}, s32[]{:T(128)}) while((s32[]{:T(128)}, bf16[2,2,384,384]{3,2,1,0:T(8,128)(2,1)}, s32[8,4]{0,1:T(4,128)S(1)}, bf16[8,2,2,128,128]{4,3,2,1,0:T(8,128)(2,1)S(1)}, s32[]{:T(128)}) %tuple.93), condition=%wide.while_cond, body=%wide.while_body.sunk | while | flops 2 | bytes 262269 | solution.py:96
  112.7 2.4 bitcast_dynamic-update-slice_fusion.12
  115.7 2.4 bitcast_dynamic-update-slice_fusion.12
  118.8 2.4 bitcast_dynamic-update-slice_fusion.12
  121.9 2.4 bitcast_dynamic-update-slice_fusion.12
  125.0 2.4 bitcast_dynamic-update-slice_fusion.12
  128.0 2.4 bitcast_dynamic-update-slice_fusion.12
  131.1 2.4 bitcast_dynamic-update-slice_fusion.12
  134.2 2.4 bitcast_dynamic-update-slice_fusion.12
  137.7 4.2 %all-to-all-start = ((bf16[8,1,2,2,128,128]{5,4,3,2,1,0:T(8,128)(2,1)}), bf16[8,1,2,2,128,128]{5,4,3,2,1,0:T(8,128)(2,1)S(1)}, u32[]{:S(2)}, u32[]{:S(2)}) async-start(bf16[8,1,2,2,128,128]{5,4,3,2,1,0:T(8,128)(2,1)} %bitcast_select_fusion.3), calls=%async_computation | async-start | bytes 2097152 | tf_op jit(solution)/shard_map/all_to_all | solution.py:151
  145.3 24.1 %while.5 = (s32[]{:T(128)}, bf16[2,2,384,384]{3,2,1,0:T(8,128)(2,1)}, s32[8,4]{0,1:T(4,128)S(1)}, bf16[8,2,2,128,128]{4,3,2,1,0:T(8,128)(2,1)S(1)}, s32[]{:T(128)}) while((s32[]{:T(128)}, bf16[2,2,384,384]{3,2,1,0:T(8,128)(2,1)}, s32[8,4]{0,1:T(4,128)S(1)}, bf16[8,2,2,128,128]{4,3,2,1,0:T(8,128)(2,1)S(1)}, s32[]{:T(128)}) %tuple.105), condition=%wide.while_cond.1, body=%wide.while_body.1.sunk | while | flops 2 | bytes 262269 | solution.py:96
  146.0 2.3 bitcast_dynamic-update-slice_fusion.13
  149.0 2.3 bitcast_dynamic-update-slice_fusion.13
  152.0 2.3 bitcast_dynamic-update-slice_fusion.13
  155.0 2.3 bitcast_dynamic-update-slice_fusion.13
  158.0 2.3 bitcast_dynamic-update-slice_fusion.13
  161.0 2.3 bitcast_dynamic-update-slice_fusion.13
  164.0 2.3 bitcast_dynamic-update-slice_fusion.13
  167.0 2.3 bitcast_dynamic-update-slice_fusion.13
  171.5 29.4 %while.6 = (s32[]{:T(128)}, bf16[2,2,384,384]{3,2,1,0:T(8,128)(2,1)}, s32[8,4]{0,1:T(4,128)S(1)}, bf16[8,2,2,128,128]{4,3,2,1,0:T(8,128)(2,1)}, s32[]{:T(128)}) while((s32[]{:T(128)}, bf16[2,2,384,384]{3,2,1,0:T(8,128)(2,1)}, s32[8,4]{0,1:T(4,128)S(1)}, bf16[8,2,2,128,128]{4,3,2,1,0:T(8,128)(2,1)}, s32[]{:T(128)}) %tuple.106), condition=%wide.while_cond.2, body=%wide.while_body.2.sunk | while | flops 2 | bytes 263793 | solution.py:96
  172.1 3.0 bitcast_dynamic-update-slice_fusion.14
  175.8 3.0 bitcast_dynamic-update-slice_fusion.14
  179.5 3.0 bitcast_dynamic-update-slice_fusion.14
  183.2 3.0 bitcast_dynamic-update-slice_fusion.14
  186.8 3.0 bitcast_dynamic-update-slice_fusion.14
  190.5 3.0 bitcast_dynamic-update-slice_fusion.14
  194.2 3.0 bitcast_dynamic-update-slice_fusion.14
  197.9 3.0 bitcast_dynamic-update-slice_fusion.14
  203.7 23.7 %while.7 = (s32[]{:T(128)}, bf16[2,2,384,384]{3,2,1,0:T(8,128)(2,1)}, s32[8,4]{0,1:T(4,128)S(1)}, bf16[8,2,2,128,128]{4,3,2,1,0:T(8,128)(2,1)S(1)}, s32[]{:T(128)}) while((s32[]{:T(128)}, bf16[2,2,384,384]{3,2,1,0:T(8,128)(2,1)}, s32[8,4]{0,1:T(4,128)S(1)}, bf16[8,2,2,128,128]{4,3,2,1,0:T(8,128)(2,1)S(1)}, s32[]{:T(128)}) %tuple.107), condition=%wide.while_cond.3, body=%wide.while_body.3.sunk | while | flops 2 | bytes 262269 | solution.py:96
  204.3 2.3 bitcast_dynamic-update-slice_fusion.15
  207.3 2.3 bitcast_dynamic-update-slice_fusion.15
  210.2 2.3 bitcast_dynamic-update-slice_fusion.15
  213.2 2.3 bitcast_dynamic-update-slice_fusion.15
  216.2 2.3 bitcast_dynamic-update-slice_fusion.15
  222.1 2.3 bitcast_dynamic-update-slice_fusion.15
  225.1 2.3 bitcast_dynamic-update-slice_fusion.15
  227.4 7.4 %all-to-all-start.1 = ((bf16[8,1,2,2,128,128]{5,4,3,2,1,0:T(8,128)(2,1)}), bf16[8,1,2,2,128,128]{5,4,3,2,1,0:T(8,128)(2,1)}, u32[]{:S(2)}, u32[]{:S(2)}) async-start(bf16[8,1,2,2,128,128]{5,4,3,2,1,0:T(8,128)(2,1)} %bitcast_select_fusion.2), calls=%async_computation.1 | async-start | bytes 2097152 | tf_op jit(solution)/shard_map/all_to_all | solution.py:151
  263.5 2.3 bitcast_select_fusion.1
  265.9 7.2 %all-to-all-start.2 = ((bf16[8,1,2,2,128,128]{5,4,3,2,1,0:T(8,128)(2,1)}), bf16[8,1,2,2,128,128]{5,4,3,2,1,0:T(8,128)(2,1)S(1)}, u32[]{:S(2)}, u32[]{:S(2)}) async-start(bf16[8,1,2,2,128,128]{5,4,3,2,1,0:T(8,128)(2,1)} %bitcast_select_fusion.1), calls=%async_computation.2 | async-start | bytes 2097152 | tf_op jit(solution)/shard_map/all_to_all | solution.py:151
  275.2 4.0 %collective-permute-done = f32[8,2,128,128]{3,2,0,1:T(8,128)} collective-permute-done((f32[8,2,128,128]{3,2,0,1:T(8,128)S(1)}, f32[8,2,128,128]{3,2,0,1:T(8,128)}, u32[]{:S(2)}, u32[]{:S(2)}) %collective-permute-start) | collective-permute-done | bytes 1048608 | tf_op jit(solution)/shard_map/ppermute | solution.py:17
  310.7 7.2 %all-to-all-start.3 = ((bf16[8,1,2,2,128,128]{5,4,3,2,1,0:T(8,128)(2,1)}), bf16[8,1,2,2,128,128]{5,4,3,2,1,0:T(8,128)(2,1)S(1)}, u32[]{:S(2)}, u32[]{:S(2)}) async-start(bf16[8,1,2,2,128,128]{5,4,3,2,1,0:T(8,128)(2,1)} %bitcast_select_fusion), calls=%async_computation.3 | async-start | bytes 2097152 | tf_op jit(solution)/shard_map/all_to_all | solution.py:151
  318.8 6.5 %collective-permute-done.1 = f32[8,2,128,128]{3,2,0,1:T(8,128)} collective-permute-done((f32[8,2,128,128]{3,2,0,1:T(8,128)}, f32[8,2,128,128]{3,2,0,1:T(8,128)}, u32[]{:S(2)}, u32[]{:S(2)}) %collective-permute-start.1) | collective-permute-done | bytes 1048608 | tf_op jit(solution)/shard_map/ppermute | solution.py:17
  356.5 14.8 %collective-permute-done.2 = f32[8,2,128,128]{3,2,0,1:T(8,128)S(1)} collective-permute-done((f32[8,2,128,128]{3,2,0,1:T(8,128)}, f32[8,2,128,128]{3,2,0,1:T(8,128)S(1)}, u32[]{:S(2)}, u32[]{:S(2)}) %collective-permute-start.2) | collective-permute-done | bytes 1048608 | tf_op jit(solution)/shard_map/ppermute | solution.py:17
  (266 shorter events, 163.1 us)
Async XLA Ops:
  137.7 89.7 %all-to-all-start = ((bf16[8,1,2,2,128,128]{5,4,3,2,1,0:T(8,128)(2,1)}), bf16[8,1,2,2,128,128]{5,4,3,2,1,0:T(8,128)(2,1)S(1)}, u32[]{:S(2)}, u32[]{:S(2)}) async-start(bf16[8,1,2,2,128,128]{5,4,3,2,1,0:T(8,128)(2,1)} %bitcast_select_fusion.3), calls=%async_computation | async-start | bytes 2097152 | tf_op jit(solution)/shard_map/all_to_all | solution.py:151
  227.4 7.4 %copy-start = (bf16[8,2,2,128,128]{4,3,2,1,0:T(8,128)(2,1)}, bf16[8,2,2,128,128]{4,3,2,1,0:T(8,128)(2,1)S(1)}, u32[]{:S(2)}) copy-start(bf16[8,2,2,128,128]{4,3,2,1,0:T(8,128)(2,1)S(1)} %get-tuple-element.37) | copy-start | bytes 3145732
  227.4 38.4 %all-to-all-start.1 = ((bf16[8,1,2,2,128,128]{5,4,3,2,1,0:T(8,128)(2,1)}), bf16[8,1,2,2,128,128]{5,4,3,2,1,0:T(8,128)(2,1)}, u32[]{:S(2)}, u32[]{:S(2)}) async-start(bf16[8,1,2,2,128,128]{5,4,3,2,1,0:T(8,128)(2,1)} %bitcast_select_fusion.2), calls=%async_computation.1 | async-start | bytes 2097152 | tf_op jit(solution)/shard_map/all_to_all | solution.py:151
  260.9 18.3 %collective-permute-start = (f32[8,2,128,128]{3,2,0,1:T(8,128)S(1)}, f32[8,2,128,128]{3,2,0,1:T(8,128)}, u32[]{:S(2)}, u32[]{:S(2)}) collective-permute-start(f32[8,2,128,128]{3,2,0,1:T(8,128)S(1)} %pad_maximum_fusion), channel_id=1, source_target_pairs={{0,8},{8,16},{16,24},{24,32},{32,40},{40,48},{48,56},{56,64},{64,7... | collective-permute-start | bytes 3145736 | tf_op jit(solution)/shard_map/ppermute | solution.py:17
  265.9 44.8 %all-to-all-start.2 = ((bf16[8,1,2,2,128,128]{5,4,3,2,1,0:T(8,128)(2,1)}), bf16[8,1,2,2,128,128]{5,4,3,2,1,0:T(8,128)(2,1)S(1)}, u32[]{:S(2)}, u32[]{:S(2)}) async-start(bf16[8,1,2,2,128,128]{5,4,3,2,1,0:T(8,128)(2,1)} %bitcast_select_fusion.1), calls=%async_computation.2 | async-start | bytes 2097152 | tf_op jit(solution)/shard_map/all_to_all | solution.py:151
  275.0 4.2 %copy-start.2 = (f32[2,128,128]{2,1,0:T(8,128)S(1)}, f32[2,128,128]{2,1,0:T(8,128)}, u32[]{:S(2)}) copy-start(f32[2,128,128]{2,1,0:T(8,128)} %param.8) | copy-start | bytes 393220
  305.7 3.8 copy-start.1
  306.8 18.5 %collective-permute-start.1 = (f32[8,2,128,128]{3,2,0,1:T(8,128)}, f32[8,2,128,128]{3,2,0,1:T(8,128)}, u32[]{:S(2)}, u32[]{:S(2)}) collective-permute-start(f32[8,2,128,128]{3,2,0,1:T(8,128)} %pad_maximum_fusion.1), channel_id=1, source_target_pairs={{0,8},{8,16},{16,24},{24,32},{32,40},{40,48},{48,56},{56,64},{64,7... | collective-permute-start | bytes 3145736 | tf_op jit(solution)/shard_map/ppermute | solution.py:17
  310.7 44.9 %all-to-all-start.3 = ((bf16[8,1,2,2,128,128]{5,4,3,2,1,0:T(8,128)(2,1)}), bf16[8,1,2,2,128,128]{5,4,3,2,1,0:T(8,128)(2,1)S(1)}, u32[]{:S(2)}, u32[]{:S(2)}) async-start(bf16[8,1,2,2,128,128]{5,4,3,2,1,0:T(8,128)(2,1)} %bitcast_select_fusion), calls=%async_computation.3 | async-start | bytes 2097152 | tf_op jit(solution)/shard_map/all_to_all | solution.py:151
  352.8 18.4 %collective-permute-start.2 = (f32[8,2,128,128]{3,2,0,1:T(8,128)}, f32[8,2,128,128]{3,2,0,1:T(8,128)S(1)}, u32[]{:S(2)}, u32[]{:S(2)}) collective-permute-start(f32[8,2,128,128]{3,2,0,1:T(8,128)} %pad_maximum_fusion.2), channel_id=1, source_target_pairs={{0,8},{8,16},{16,24},{24,32},{32,40},{40,48},{48,56},{56,64},{64,7... | collective-permute-start | bytes 3145736 | tf_op jit(solution)/shard_map/ppermute | solution.py:17
where the time goes:
time: 404 us; the launch traced here: 398 us
  local copies, waits for them, and re-layouts  118 us (29%)
  blocking collectives  100 us (25%)
  matrix products  99.2 us (25%)
  starting transfers between devices  31.7 us (8%)
  waiting for transfers between devices  25.3 us (6%)
  other arithmetic  21 us (5%)
    gather x96, local copies, waits for them, and re-layouts  101 us
    dot_general x96, matrix products, plane_dot(): jnp.dot(flat, table, precision=lax.Precision.HIGHEST, preferred_element_t...  99.2 us
    all_gather x4, blocking collectives, per_device(): lax.all_gather(listing[None], 'tile', axis=0, tiled=True)  84.3 us
    all_to_all x4, starting transfers between devices, per_device(): lax.all_to_all(outgoing(got_lists, got_counts), 'tile', split_axis=0, con...  26 us
    ppermute x3, waiting for transfers between devices, from_behind(): lax.ppermute(value, axis, [(source, source + steps) for source in range(l...  25.3 us
    all_gather x1, blocking collectives, per_device(): lax.all_gather(count[None], 'tile', axis=0, tiled=True)  16.1 us
    unnamed x23, local copies, waits for them, and re-layouts  8.72 us
  transfers between devices with their start and end apart: 7, of which 3 were waited for; matrix products, arithmetic and copies ran while one was open for 44% of the time, Pallas kernels for 0%

commit v1 on v0

v1 whole, which is shorter than its diff:
```python
import functools
import math

import jax
import jax.numpy as jnp
import ml_dtypes
import numpy as np
from jax import lax
from jax.experimental import pallas as pl
from jax.experimental.pallas import tpu as pltpu
from jax.sharding import PartitionSpec as P

STEPS = 4
FRESNEL_RATE = 0.3
MESH = pl.DeviceIdType.MESH

ROWS = 272
TOP = 32766.0


def split_table(table):
    high = table.astype(ml_dtypes.bfloat16)
    low = (table - high.astype(np.float64)).astype(ml_dtypes.bfloat16)
    return high, low


def propagator(width):
    index = np.arange(width)
    angle = 2.0 * math.pi / width * ((index[:, None] * index[None, :]) % width)
    forward = np.cos(angle) - 1j * np.sin(angle)
    inverse = (np.cos(angle) + 1j * np.sin(angle)) / width
    freq = np.where(index < width // 2, index, index - width).astype(np.float64)
    phase = -2.0 * math.pi * FRESNEL_RATE / width * freq**2
    matrix = inverse @ ((np.cos(phase) + 1j * np.sin(phase))[:, None] * forward)
    real, imag = matrix.real, matrix.imag
    right = np.block([[real, imag], [-imag, real]])
    left = np.block([[real, -imag], [imag, real]])
    return split_table(right) + split_table(left)


def offset_of(slot):
    return lax.rem(8 + (lax.rem(slot, 2) * 2 - 1) * ((slot + 1) // 2), 8)


def encode(plane):
    groups = plane.reshape(16, 8, 128)
    largest = jnp.maximum(jnp.max(jnp.abs(groups), axis=0), 1e-30)
    power = jnp.ceil(jnp.log2(largest) * 256.0)
    scale = jnp.exp2(power * (-1.0 / 256.0)) * TOP
    coded = jnp.round(groups * scale[None]).reshape(128, 128)
    return coded.astype(jnp.int32).astype(jnp.int16), power


def store_wave(ref, real, imag):
    coded_real, power_real = encode(real)
    coded_imag, power_imag = encode(imag)
    ref[0:128, :] = coded_real
    ref[128:256, :] = coded_imag
    powers = jnp.concatenate([power_real, power_imag], axis=0)
    ref[256:272, :] = powers.astype(jnp.int32).astype(jnp.int16)


def decode(coded):
    numbers = coded.astype(jnp.int32).astype(jnp.float32)
    scales = jnp.exp2(numbers[256:272] * (1.0 / 256.0)) * (1.0 / TOP)
    real = (numbers[0:128].reshape(16, 8, 128) * scales[0:8][None]).reshape(128, 128)
    imag = (numbers[128:256].reshape(16, 8, 128) * scales[8:16][None]).reshape(128, 128)
    return real, imag


def split(value):
    high = value.astype(jnp.bfloat16)
    return high, (value - high.astype(jnp.float32)).astype(jnp.bfloat16)


def dot(a, b):
    return jnp.dot(a, b, preferred_element_type=jnp.float32)


def kernel(
    own, fronts, probe, obj, right_high, right_low, left_high, left_low, lists, out,
    fronts_v, probe_v, obj_b, obj_f, lists_v, lists_s, send0, waves, made, back,
    local_sem, list_send, list_recv, in_send, in_recv, hop_send, hop_recv, out_send, out_recv,
):
    d = lax.axis_index("depth")
    u = lax.axis_index("tile")
    n_depth = lax.axis_size("depth")

    barrier = pltpu.get_barrier_semaphore()
    for j in range(1, 8):
        pl.semaphore_signal(barrier, inc=1, device_id=(d, lax.rem(u + j, 8)), device_id_type=MESH)
    pl.semaphore_signal(barrier, inc=1, device_id=(lax.rem(d + 1, n_depth), u), device_id_type=MESH)
    pl.semaphore_signal(barrier, inc=1, device_id=(lax.rem(d + n_depth - 1, n_depth), u), device_id_type=MESH)

    get_fronts = pltpu.make_async_copy(fronts, fronts_v, local_sem.at[0])
    get_probe = pltpu.make_async_copy(probe, probe_v, local_sem.at[1])
    get_obj = pltpu.make_async_copy(obj, obj_b, local_sem.at[2])
    get_fronts.start()
    get_probe.start()
    get_obj.start()

    get_fronts.wait()

    @pl.loop(0, 8)
    def _(j):
        wave = fronts_v[own[j]]

        @pl.when(j == 0)
        def _():
            store_wave(waves.at[0, 0], wave[0], wave[1])

        @pl.when(j > 0)
        def _():
            store_wave(send0.at[j], wave[0], wave[1])

    get_probe.wait()

    @pl.when(d == 0)
    def _():
        @pl.loop(0, 8)
        def _(j):
            for s in range(1, STEPS):
                store_wave(waves.at[s, j], probe_v[0], probe_v[1])

    pl.semaphore_wait(barrier, 9)

    def list_copy(j):
        return pltpu.make_async_remote_copy(
            lists.at[j], lists_v.at[j], list_send.at[j], list_recv.at[j],
            device_id=(d, lax.rem(u + 8 - offset_of(j), 8)), device_id_type=MESH)

    def in_copy(j):
        return pltpu.make_async_remote_copy(
            send0.at[j], waves.at[0, j], in_send.at[j], in_recv.at[j],
            device_id=(d, lax.rem(u + 8 - offset_of(j), 8)), device_id_type=MESH)

    def hop_copy(s, pair):
        return pltpu.make_async_remote_copy(
            made.at[s, pl.ds(2 * pair, 2)], waves.at[s + 1, pl.ds(2 * pair, 2)],
            hop_send.at[s, pair], hop_recv.at[s, pair],
            device_id=(lax.rem(d + 1, n_depth), u), device_id_type=MESH)

    def out_copy(j):
        return pltpu.make_async_remote_copy(
            made.at[3, j], back.at[j], out_send.at[j], out_recv.at[j],
            device_id=(d, lax.rem(u + offset_of(j), 8)), device_id_type=MESH)

    @pl.loop(1, 8)
    def _(j):
        list_copy(j).start()

    @pl.loop(1, 8)
    def _(j):
        in_copy(j).start()

    lists_v[0] = lists[0]

    get_obj.wait()
    for layer in range(2):
        for part in range(2):
            for third in range(3):
                obj_f[layer, part, third] = obj_b[layer, part, :, third * 128:(third + 1) * 128].astype(jnp.float32)

    @pl.loop(1, 8)
    def _(j):
        list_copy(j).wait()

    get_lists = pltpu.make_async_copy(lists_v, lists_s, local_sem.at[3])
    get_lists.start()
    get_lists.wait()

    lane = lax.broadcasted_iota(jnp.int32, (128, 128), 1)

    def cut(layer, part, row, column):
        third = lax.shift_right_logical(column, 7)
        left = lax.bitwise_and(column, 127)
        first = obj_f[layer, part, third, pl.ds(row, 128), :]
        second = obj_f[layer, part, jnp.minimum(third + 1, 2), pl.ds(row, 128), :]
        mixed = jnp.where(lane >= left, first, second)
        return pltpu.roll(mixed, lax.bitwise_and(128 - left, 127), 1)

    def one_task(s, pair):
        @pl.when(s == 0)
        def _():
            @pl.when(pair > 0)
            def _():
                in_copy(2 * pair).wait_recv()

            in_copy(2 * pair + 1).wait_recv()

        @pl.when((s > 0) & (d > 0))
        def _():
            hop_copy(s - 1, pair).wait_recv()

        real = [None, None]
        imag = [None, None]
        for side in range(2):
            real[side], imag[side] = decode(waves[s, 2 * pair + side])
        for layer in range(2):
            for side in range(2):
                row = lists_s[2 * pair + side, 0, s]
                column = lists_s[2 * pair + side, 0, 4 + s]
                trans_real = cut(layer, 0, row, column)
                trans_imag = cut(layer, 1, row, column)
                real[side], imag[side] = (
                    real[side] * trans_real - imag[side] * trans_imag,
                    real[side] * trans_imag + imag[side] * trans_real,
                )
            high, low = split(jnp.concatenate([
                jnp.concatenate([real[0], imag[0]], axis=1),
                jnp.concatenate([real[1], imag[1]], axis=1),
            ], axis=0))
            got = dot(high, right_high[...]) + dot(high, right_low[...]) + dot(low, right_high[...])
            high, low = split(jnp.concatenate([
                jnp.concatenate([got[0:128, 0:128], got[128:256, 0:128]], axis=1),
                jnp.concatenate([got[0:128, 128:256], got[128:256, 128:256]], axis=1),
            ], axis=0))
            got = dot(left_high[...], high) + dot(left_low[...], high) + dot(left_high[...], low)
            for side in range(2):
                real[side] = got[0:128, side * 128:(side + 1) * 128]
                imag[side] = got[128:256, side * 128:(side + 1) * 128]
        for side in range(2):
            store_wave(made.at[s, 2 * pair + side], real[side], imag[side])

        @pl.when((s < 3) & (d < n_depth - 1))
        def _():
            hop_copy(s, pair).start()

        @pl.when(s == 3)
        def _():
            @pl.when(pair > 0)
            def _():
                out_copy(2 * pair).start()

            @pl.when(pair == 0)
            def _():
                back[0] = made[3, 0]

            out_copy(2 * pair + 1).start()

    @pl.loop(0, 7)
    def _(g):
        @pl.loop(0, 4)
        def _(i):
            s = 3 - i
            pair = g - s

            @pl.when((pair >= 0) & (pair < 4))
            def _():
                one_task(s, pair)

    @pl.loop(1, 8)
    def _(j):
        in_copy(j).wait_send()
        out_copy(j).wait()

    @pl.when(d < n_depth - 1)
    def _():
        @pl.loop(0, 3)
        def _(s):
            @pl.loop(0, 4)
            def _(pair):
                hop_copy(s, pair).wait_send()

    @pl.loop(0, 8)
    def _(p):
        real, imag = decode(back[own[8 + p]])
        live = own[16 + p] > 0
        out[p, 0] = jnp.where(live, real, 0.0)
        out[p, 1] = jnp.where(live, imag, 0.0)


def per_device(fronts, probe_wave, object_slices, patch_list, counts):
    d = lax.axis_index("depth")
    t = lax.axis_index("tile")
    first = lax.axis_size("depth") - 1 - d
    listed = lax.dynamic_slice(patch_list[:, 0], (first, 0, 0), (STEPS, 3, 8))
    count = lax.dynamic_slice(counts[:, 0], (first,), (STEPS,))
    probes = jnp.arange(8, dtype=jnp.int32)
    offset = lax.rem(t - listed[:, 0] + 8, 8)
    slot = jnp.where(offset == 0, 0, jnp.where(offset <= 4, 2 * offset - 1, 16 - 2 * offset))
    live = probes[None] < count[:, None]
    chosen = (live[:, None] & (slot[:, None] == probes[None, :, None])).astype(jnp.int32)
    rows = jnp.sum(chosen * listed[:, 1][:, None], axis=-1)
    columns = jnp.sum(chosen * listed[:, 2][:, None], axis=-1)
    source = jnp.sum(chosen[0] * probes[None], axis=-1)
    own = jnp.concatenate([source, slot[3], live[3].astype(jnp.int32)])
    lists = jnp.concatenate([rows, columns], axis=0).T
    lists = jnp.pad(lists[:, None, :], ((0, 0), (0, 7), (0, 120)))
    tables = propagator(128)
    any_space = pl.BlockSpec(memory_space=pl.ANY)
    vmem = pl.BlockSpec(memory_space=pltpu.VMEM)
    result = pl.pallas_call(
        kernel,
        out_shape=jax.ShapeDtypeStruct((8, 2, 128, 128), jnp.float32),
        in_specs=[pl.BlockSpec(memory_space=pltpu.SMEM), any_space, any_space, any_space, vmem, vmem, vmem, vmem, vmem],
        out_specs=vmem,
        scratch_shapes=[
            pltpu.VMEM((8, 2, 128, 128), jnp.float32),
            pltpu.VMEM((2, 128, 128), jnp.float32),
            pltpu.VMEM((2, 2, 384, 384), jnp.bfloat16),
            pltpu.VMEM((2, 2, 3, 384, 128), jnp.float32),
            pltpu.VMEM((8, 8, 128), jnp.int32),
            pltpu.SMEM((8, 8, 128), jnp.int32),
            pltpu.VMEM((8, ROWS, 128), jnp.int16),
            pltpu.VMEM((STEPS, 8, ROWS, 128), jnp.int16),
            pltpu.VMEM((STEPS, 8, ROWS, 128), jnp.int16),
            pltpu.VMEM((8, ROWS, 128), jnp.int16),
            pltpu.SemaphoreType.DMA((4,)),
            pltpu.SemaphoreType.DMA((8,)),
            pltpu.SemaphoreType.DMA((8,)),
            pltpu.SemaphoreType.DMA((8,)),
            pltpu.SemaphoreType.DMA((8,)),
            pltpu.SemaphoreType.DMA((3, 4)),
            pltpu.SemaphoreType.DMA((3, 4)),
            pltpu.SemaphoreType.DMA((8,)),
            pltpu.SemaphoreType.DMA((8,)),
        ],
        compiler_params=pltpu.CompilerParams(
            collective_id=0, has_side_effects=True, vmem_limit_bytes=40 * 1024 * 1024
        ),
    )(own, fronts[0, 0], probe_wave, object_slices, *[jnp.asarray(x) for x in tables], lists)
    return result[None, None]


def solution(mesh):
    in_specs = (
        P("depth", "tile", None, None, None, None),
        P(),
        P("depth", None, "tile", None),
        P(None, "tile", None, None),
        P(None, "tile"),
    )
    out_specs = P("depth", "tile", None, None, None, None)
    return jax.shard_map(
        per_device, mesh=mesh, in_specs=in_specs, out_specs=out_specs, check_vma=False
    )
```

time: 404 us -> 63.8 us (0.16)
  the two profiles are of different devices: /device:TPU:6 before, /device:TPU:102 now
where the time goes in v1:
time: 63.8 us; the launch traced here: 63.5 us
  Pallas kernels  54 us (85%)
  local copies, waits for them, and re-layouts  8.98 us (14%)
    pallas_call x1, Pallas kernels, per_device(): pl.pallas_call(kernel, out_shape=jax.ShapeDtypeStruct((8, 2, 128, 128), j...  54 us
    unnamed x17, local copies, waits for them, and re-layouts  7.99 us

profile of v1, /device:TPU:102, one launch (start us, length us, event | category | flops | bytes accessed | tf_op | source)
XLA Modules:
  0.0 63.5 jit_solution(13762810820427898284)
XLA Ops:
  0.0 0.0 copy-start
  0.0 0.7 %dynamic-slice_bitcast_fusion = s32[4]{0:T(128)S(1)} fusion(s32[35,1]{0,1:T(1,128)} %param.13, s32[]{:T(128)S(6)} %select_n.18), kind=kLoop, calls=%fused_computation.24 | loop fusion | bytes 36 | tf_op jit(solution)/shard_map/lt | solution.py:282
  0.7 0.1 iota_compare_fusion.1
  0.8 0.0 copy-done
  0.8 0.1 constant_dynamic-slice_fusion
  0.9 0.1 copy.12
  1.0 0.2 select_reduce_fusion.1
  1.3 0.1 copy.14
  1.4 0.1 select_reduce_fusion.2
  1.5 0.1 pad_add_fusion.own
  1.6 0.0 copy-start.1
  1.6 1.3 %copy-done.1 = bf16[2,2,384,384]{3,2,1,0:T(8,128)(2,1)S(1)} copy-done((bf16[2,2,384,384]{3,2,1,0:T(8,128)(2,1)S(1)}, bf16[2,2,384,384]{3,2,1,0:T(8,128)(2,1)}, u32[]{:S(2)}) %copy-start.1) | copy-done | bytes 1179672
  2.8 0.0 copy-start.2
  2.8 1.2 %copy-done.2 = f32[1,1,8,2,128,128]{5,4,3,2,1,0:T(8,128)S(1)} copy-done((f32[1,1,8,2,128,128]{5,4,3,2,1,0:T(8,128)S(1)}, f32[1,1,8,2,128,128]{5,4,3,2,1,0:T(8,128)}, u32[]{:S(2)}) %copy-start.2) | copy-done | bytes 1048600
  4.1 0.0 copy-start.3
  4.1 0.9 %copy-done.3 = f32[2,128,128]{2,1,0:T(8,128)S(1)} copy-done((f32[2,128,128]{2,1,0:T(8,128)S(1)}, f32[2,128,128]{2,1,0:T(8,128)}, u32[]{:S(2)}) %copy-start.3) | copy-done | bytes 131096
  5.0 0.0 copy-start.4
  5.0 0.9 %copy-done.4 = bf16[256,256]{1,0:T(8,128)(2,1)S(1)} copy-done((bf16[256,256]{1,0:T(8,128)(2,1)S(1)}, bf16[256,256]{1,0:T(8,128)(2,1)}, u32[]{:S(2)}) %copy-start.4) | copy-done | bytes 131096
  5.9 0.0 copy-start.5
  5.9 0.9 %copy-done.5 = bf16[256,256]{1,0:T(8,128)(2,1)S(1)} copy-done((bf16[256,256]{1,0:T(8,128)(2,1)S(1)}, bf16[256,256]{1,0:T(8,128)(2,1)}, u32[]{:S(2)}) %copy-start.5) | copy-done | bytes 131096
  6.8 0.0 copy-start.6
  6.8 0.9 %copy-done.6 = bf16[256,256]{1,0:T(8,128)(2,1)S(1)} copy-done((bf16[256,256]{1,0:T(8,128)(2,1)S(1)}, bf16[256,256]{1,0:T(8,128)(2,1)}, u32[]{:S(2)}) %copy-start.6) | copy-done | bytes 131096
  7.7 0.0 copy-start.7
  7.7 0.9 %copy-done.7 = bf16[256,256]{1,0:T(8,128)(2,1)S(1)} copy-done((bf16[256,256]{1,0:T(8,128)(2,1)S(1)}, bf16[256,256]{1,0:T(8,128)(2,1)}, u32[]{:S(2)}) %copy-start.7) | copy-done | bytes 131096
  8.6 54.0 %shard_map.91 = f32[8,2,128,128]{3,2,1,0:T(8,128)S(1)} custom-call(s32[24]{0:T(128)S(1)} %pad_add_fusion.own, f32[8,2,128,128]{3,2,1,0:T(8,128)S(1)} %bitcast.28, f32[2,128,128]{2,1,0:T(8,128)S(1)} %copy-done.3, bf16[2,2,384,384]{3,2,1,0:T(8,128)(2,1)S(1)} %copy-done.1, bf16[256,256]{1,0:T(8,128)(2,1)S(1)} %copy-done.7, bf16[256,256]{1,0:T(8,128)(2,1)S(1)} %copy-done.6, ...), custom_call_target="tpu_custom_call" | custom-call | tf_op jit(solution)/shard_map/pallas_call | solution.py:293
  62.6 1.0 %copy.18 = f32[1,1,8,2,128,128]{5,4,3,2,1,0:T(8,128)} copy(f32[1,1,8,2,128,128]{5,4,3,2,1,0:T(8,128)S(1)} %bitcast.27) | data formatting | bytes 2097152
  (7 shorter events, 0.1 us)
Async XLA Ops:
  0.0 0.8 %copy-start = (s32[35,1,3,8]{0,3,2,1:T(8,128)S(1)}, s32[35,1,3,8]{0,3,2,1:T(8,128)}, u32[]{:S(2)}) copy-start(s32[35,1,3,8]{0,3,2,1:T(8,128)} %param.12) | copy-start | bytes 10084
  1.6 1.3 %copy-start.1 = (bf16[2,2,384,384]{3,2,1,0:T(8,128)(2,1)S(1)}, bf16[2,2,384,384]{3,2,1,0:T(8,128)(2,1)}, u32[]{:S(2)}) copy-start(bf16[2,2,384,384]{3,2,1,0:T(8,128)(2,1)} %obj.1) | copy-start | bytes 3538948
  2.8 1.2 %copy-start.2 = (f32[1,1,8,2,128,128]{5,4,3,2,1,0:T(8,128)S(1)}, f32[1,1,8,2,128,128]{5,4,3,2,1,0:T(8,128)}, u32[]{:S(2)}) copy-start(f32[1,1,8,2,128,128]{5,4,3,2,1,0:T(8,128)} %param.9) | copy-start | bytes 3145732
  4.1 0.9 %copy-start.3 = (f32[2,128,128]{2,1,0:T(8,128)S(1)}, f32[2,128,128]{2,1,0:T(8,128)}, u32[]{:S(2)}) copy-start(f32[2,128,128]{2,1,0:T(8,128)} %probe.1) | copy-start | bytes 393220
  5.0 0.9 %copy-start.4 = (bf16[256,256]{1,0:T(8,128)(2,1)S(1)}, bf16[256,256]{1,0:T(8,128)(2,1)}, u32[]{:S(2)}) copy-start(bf16[256,256]{1,0:T(8,128)(2,1)} %constant.47.clone.left_low) | copy-start | bytes 393220
  5.9 0.9 %copy-start.5 = (bf16[256,256]{1,0:T(8,128)(2,1)S(1)}, bf16[256,256]{1,0:T(8,128)(2,1)}, u32[]{:S(2)}) copy-start(bf16[256,256]{1,0:T(8,128)(2,1)} %constant.46.clone.left_high) | copy-start | bytes 393220
  6.8 0.9 %copy-start.6 = (bf16[256,256]{1,0:T(8,128)(2,1)S(1)}, bf16[256,256]{1,0:T(8,128)(2,1)}, u32[]{:S(2)}) copy-start(bf16[256,256]{1,0:T(8,128)(2,1)} %constant.45.clone.right_low) | copy-start | bytes 393220
  7.7 0.9 %copy-start.7 = (bf16[256,256]{1,0:T(8,128)(2,1)S(1)}, bf16[256,256]{1,0:T(8,128)(2,1)}, u32[]{:S(2)}) copy-start(bf16[256,256]{1,0:T(8,128)(2,1)} %constant.44.clone.right_high) | copy-start | bytes 393220

commit v2 on v1

--- a/solution.py
+++ b/solution.py
@@ -39,7 +39,14 @@
 
 
 def offset_of(slot):
-    return lax.rem(8 + (lax.rem(slot, 2) * 2 - 1) * ((slot + 1) // 2), 8)
+    pair = slot // 2
+    return lax.rem(16 + (lax.rem(pair, 2) * 2 - 1) * ((pair + 1) // 2) + 4 * lax.rem(slot, 2), 8)
+
+
+def slot_of(offset):
+    side = jnp.where((offset >= 3) & (offset <= 6), 1, 0)
+    base = (offset + 4 * side) % 8
+    return 2 * jnp.where(base == 7, 2, jnp.where(base == 2, 3, base)) + side
 
 
 def encode(plane):
@@ -78,13 +85,15 @@
 
 
 def kernel(
-    own, fronts, probe, obj, right_high, right_low, left_high, left_low, lists, out,
-    fronts_v, probe_v, obj_b, obj_f, lists_v, lists_s, send0, waves, made, back,
+    listed, counts, fronts, probe, obj, tables, out,
+    listed_s, counts_s, listed_v, counts_v, tables_v, fronts_v, probe_v, obj_b, obj_f,
+    lists, lists_v, lists_s, send0, waves, made, back,
     local_sem, list_send, list_recv, in_send, in_recv, hop_send, hop_recv, out_send, out_recv,
 ):
     d = lax.axis_index("depth")
     u = lax.axis_index("tile")
     n_depth = lax.axis_size("depth")
+    batches = listed.shape[-1]
 
     barrier = pltpu.get_barrier_semaphore()
     for j in range(1, 8):
@@ -92,18 +101,35 @@
     pl.semaphore_signal(barrier, inc=1, device_id=(lax.rem(d + 1, n_depth), u), device_id_type=MESH)
     pl.semaphore_signal(barrier, inc=1, device_id=(lax.rem(d + n_depth - 1, n_depth), u), device_id_type=MESH)
 
-    get_fronts = pltpu.make_async_copy(fronts, fronts_v, local_sem.at[0])
-    get_probe = pltpu.make_async_copy(probe, probe_v, local_sem.at[1])
-    get_obj = pltpu.make_async_copy(obj, obj_b, local_sem.at[2])
-    get_fronts.start()
-    get_probe.start()
-    get_obj.start()
-
-    get_fronts.wait()
+    pairs = ((listed, listed_v), (counts, counts_v), (listed, listed_s), (counts, counts_s), (fronts, fronts_v),
+             (probe, probe_v), (obj, obj_b), (tables, tables_v))
+    gets = [pltpu.make_async_copy(a, b, local_sem.at[i]) for i, (a, b) in enumerate(pairs)]
+    for get in gets:
+        get.start()
+
+    first = n_depth - 1 - d
+    gets[0].wait()
+    gets[1].wait()
+    probes = lax.broadcasted_iota(jnp.int32, (8, batches), 0)
+    live = probes < counts_v[...]
+    slots = jnp.where(live, slot_of(lax.rem(u - listed_v[0] + 8, 8)), -1)
+    for j in range(8):
+        chosen = slots == j
+        for field in range(2):
+            lists[j, field:field + 1, :] = jnp.sum(
+                jnp.where(chosen, listed_v[1 + field], 0), axis=0, keepdims=True)
+
+    for get in gets[2:5]:
+        get.wait()
 
     @pl.loop(0, 8)
     def _(j):
-        wave = fronts_v[own[j]]
+        target = lax.rem(u + 8 - offset_of(j), 8)
+        count = counts_s[0, first]
+        source = jnp.int32(0)
+        for p in range(8):
+            source = jnp.where((listed_s[0, p, first] == target) & (p < count), p, source)
+        wave = fronts_v[source]
 
         @pl.when(j == 0)
         def _():
@@ -113,7 +139,7 @@
         def _():
             store_wave(send0.at[j], wave[0], wave[1])
 
-    get_probe.wait()
+    gets[5].wait()
 
     @pl.when(d == 0)
     def _():
@@ -155,7 +181,7 @@
 
     lists_v[0] = lists[0]
 
-    get_obj.wait()
+    gets[6].wait()
     for layer in range(2):
         for part in range(2):
             for third in range(3):
@@ -165,9 +191,10 @@
     def _(j):
         list_copy(j).wait()
 
-    get_lists = pltpu.make_async_copy(lists_v, lists_s, local_sem.at[3])
+    get_lists = pltpu.make_async_copy(lists_v, lists_s, local_sem.at[8])
     get_lists.start()
     get_lists.wait()
+    gets[7].wait()
 
     lane = lax.broadcasted_iota(jnp.int32, (128, 128), 1)
 
@@ -198,8 +225,8 @@
             real[side], imag[side] = decode(waves[s, 2 * pair + side])
         for layer in range(2):
             for side in range(2):
-                row = lists_s[2 * pair + side, 0, s]
-                column = lists_s[2 * pair + side, 0, 4 + s]
+                row = lists_s[2 * pair + side, 0, first + s]
+                column = lists_s[2 * pair + side, 1, first + s]
                 trans_real = cut(layer, 0, row, column)
                 trans_imag = cut(layer, 1, row, column)
                 real[side], imag[side] = (
@@ -210,12 +237,12 @@
                 jnp.concatenate([real[0], imag[0]], axis=1),
                 jnp.concatenate([real[1], imag[1]], axis=1),
             ], axis=0))
-            got = dot(high, right_high[...]) + dot(high, right_low[...]) + dot(low, right_high[...])
+            got = dot(high, tables_v[0]) + dot(high, tables_v[1]) + dot(low, tables_v[0])
             high, low = split(jnp.concatenate([
                 jnp.concatenate([got[0:128, 0:128], got[128:256, 0:128]], axis=1),
                 jnp.concatenate([got[0:128, 128:256], got[128:256, 128:256]], axis=1),
             ], axis=0))
-            got = dot(left_high[...], high) + dot(left_low[...], high) + dot(left_high[...], low)
+            got = dot(tables_v[2], high) + dot(tables_v[3], high) + dot(tables_v[2], low)
             for side in range(2):
                 real[side] = got[0:128, side * 128:(side + 1) * 128]
                 imag[side] = got[128:256, side * 128:(side + 1) * 128]
@@ -242,7 +269,7 @@
     def _(g):
         @pl.loop(0, 4)
         def _(i):
-            s = 3 - i
+            s = i
             pair = g - s
 
             @pl.when((pair >= 0) & (pair < 4))
@@ -264,49 +291,41 @@
 
     @pl.loop(0, 8)
     def _(p):
-        real, imag = decode(back[own[8 + p]])
-        live = own[16 + p] > 0
+        last = first + STEPS - 1
+        real, imag = decode(back[slot_of(lax.rem(u - listed_s[0, p, last] + 8, 8))])
+        live = p < counts_s[0, last]
         out[p, 0] = jnp.where(live, real, 0.0)
         out[p, 1] = jnp.where(live, imag, 0.0)
 
 
 def per_device(fronts, probe_wave, object_slices, patch_list, counts):
-    d = lax.axis_index("depth")
-    t = lax.axis_index("tile")
-    first = lax.axis_size("depth") - 1 - d
-    listed = lax.dynamic_slice(patch_list[:, 0], (first, 0, 0), (STEPS, 3, 8))
-    count = lax.dynamic_slice(counts[:, 0], (first,), (STEPS,))
-    probes = jnp.arange(8, dtype=jnp.int32)
-    offset = lax.rem(t - listed[:, 0] + 8, 8)
-    slot = jnp.where(offset == 0, 0, jnp.where(offset <= 4, 2 * offset - 1, 16 - 2 * offset))
-    live = probes[None] < count[:, None]
-    chosen = (live[:, None] & (slot[:, None] == probes[None, :, None])).astype(jnp.int32)
-    rows = jnp.sum(chosen * listed[:, 1][:, None], axis=-1)
-    columns = jnp.sum(chosen * listed[:, 2][:, None], axis=-1)
-    source = jnp.sum(chosen[0] * probes[None], axis=-1)
-    own = jnp.concatenate([source, slot[3], live[3].astype(jnp.int32)])
-    lists = jnp.concatenate([rows, columns], axis=0).T
-    lists = jnp.pad(lists[:, None, :], ((0, 0), (0, 7), (0, 120)))
-    tables = propagator(128)
+    tables = jnp.asarray(np.stack(propagator(128)))
+    batches = counts.shape[0]
     any_space = pl.BlockSpec(memory_space=pl.ANY)
     vmem = pl.BlockSpec(memory_space=pltpu.VMEM)
     result = pl.pallas_call(
         kernel,
         out_shape=jax.ShapeDtypeStruct((8, 2, 128, 128), jnp.float32),
-        in_specs=[pl.BlockSpec(memory_space=pltpu.SMEM), any_space, any_space, any_space, vmem, vmem, vmem, vmem, vmem],
+        in_specs=[any_space] * 6,
         out_specs=vmem,
         scratch_shapes=[
+            pltpu.SMEM((3, 8, batches), jnp.int32),
+            pltpu.SMEM((1, batches), jnp.int32),
+            pltpu.VMEM((3, 8, batches), jnp.int32),
+            pltpu.VMEM((1, batches), jnp.int32),
+            pltpu.VMEM((4, 256, 256), jnp.bfloat16),
             pltpu.VMEM((8, 2, 128, 128), jnp.float32),
             pltpu.VMEM((2, 128, 128), jnp.float32),
             pltpu.VMEM((2, 2, 384, 384), jnp.bfloat16),
             pltpu.VMEM((2, 2, 3, 384, 128), jnp.float32),
-            pltpu.VMEM((8, 8, 128), jnp.int32),
-            pltpu.SMEM((8, 8, 128), jnp.int32),
+            pltpu.VMEM((8, 8, batches), jnp.int32),
+            pltpu.VMEM((8, 8, batches), jnp.int32),
+            pltpu.SMEM((8, 8, batches), jnp.int32),
             pltpu.VMEM((8, ROWS, 128), jnp.int16),
             pltpu.VMEM((STEPS, 8, ROWS, 128), jnp.int16),
             pltpu.VMEM((STEPS, 8, ROWS, 128), jnp.int16),
             pltpu.VMEM((8, ROWS, 128), jnp.int16),
-            pltpu.SemaphoreType.DMA((4,)),
+            pltpu.SemaphoreType.DMA((9,)),
             pltpu.SemaphoreType.DMA((8,)),
             pltpu.SemaphoreType.DMA((8,)),
             pltpu.SemaphoreType.DMA((8,)),
@@ -317,9 +336,11 @@
             pltpu.SemaphoreType.DMA((8,)),
         ],
         compiler_params=pltpu.CompilerParams(
-            collective_id=0, has_side_effects=True, vmem_limit_bytes=40 * 1024 * 1024
+            collective_id=0, has_side_effects=True, vmem_limit_bytes=60 * 1024 * 1024
         ),
-    )(own, fronts[0, 0], probe_wave, object_slices, *[jnp.asarray(x) for x in tables], lists)
+    )(
+        jnp.transpose(patch_list[:, 0], (1, 2, 0)), jnp.transpose(counts), fronts[0, 0], probe_wave, object_slices, tables
+    )
     return result[None, None]
 
 

time: 63.8 us -> 53.5 us (0.84)
  the two profiles are of different devices: /device:TPU:102 before, /device:TPU:6 now
where the time goes in v2:
time: 53.5 us; the launch traced here: 53.3 us
  Pallas kernels  51 us (95%)
  local copies, waits for them, and re-layouts  2.3 us (4%)
    pallas_call x1, Pallas kernels, per_device(): pl.pallas_call(kernel, out_shape=jax.ShapeDtypeStruct((8, 2, 128, 128), j...  51 us
    unnamed x1, local copies, waits for them, and re-layouts  2.3 us

profile of v2, /device:TPU:6, one launch (start us, length us, event | category | flops | bytes accessed | tf_op | source)
XLA Modules:
  0.0 53.3 jit_solution(1934742070190394069)
XLA Ops:
  0.0 51.0 %shard_map.64 = f32[8,2,128,128]{3,2,1,0:T(8,128)} custom-call(s32[3,8,35]{2,1,0:T(8,128)} %bitcast.8, s32[1,35]{1,0:T(1,128)} %bitcast.9, f32[8,2,128,128]{3,2,1,0:T(8,128)} %bitcast.7, f32[2,128,128]{2,1,0:T(8,128)} %probe.1, bf16[2,2,384,384]{3,2,1,0:T(8,128)(2,1)} %obj.1, bf16[4,256,256]{2,1,0:T(8,128)(2,1)} %constant.2.clone.tables), custom_call_target="tpu_custom_call" | custom-call | tf_op jit(solution)/shard_map/pallas_call | solution.py:306
  51.0 2.3 %copy.8 = f32[1,1,8,2,128,128]{5,4,3,2,1,0:T(8,128)} copy(f32[1,1,8,2,128,128]{5,4,3,2,1,0:T(8,128)} %bitcast.6) | data formatting | bytes 2097152

commit v3 on v2

--- a/solution.py
+++ b/solution.py
@@ -85,9 +85,9 @@
 
 
 def kernel(
-    listed, counts, fronts, probe, obj, tables, out,
+    listed, counts, fronts, probe, obj, tables, back,
     listed_s, counts_s, listed_v, counts_v, tables_v, fronts_v, probe_v, obj_b, obj_f,
-    lists, lists_v, lists_s, send0, waves, made, back,
+    lists, lists_v, lists_s, send0, waves, made,
     local_sem, list_send, list_recv, in_send, in_recv, hop_send, hop_recv, out_send, out_recv,
 ):
     d = lax.axis_index("depth")
@@ -196,6 +196,7 @@
     get_lists.wait()
     gets[7].wait()
 
+    keep = pltpu.make_async_copy(made.at[3, 0], back.at[0], local_sem.at[9])
     lane = lax.broadcasted_iota(jnp.int32, (128, 128), 1)
 
     def cut(layer, part, row, column):
@@ -233,14 +234,13 @@
                     real[side] * trans_real - imag[side] * trans_imag,
                     real[side] * trans_imag + imag[side] * trans_real,
                 )
+            got = []
+            for side in range(2):
+                high, low = split(jnp.concatenate([real[side], imag[side]], axis=1))
+                got.append(dot(high, tables_v[0]) + dot(high, tables_v[1]) + dot(low, tables_v[0]))
             high, low = split(jnp.concatenate([
-                jnp.concatenate([real[0], imag[0]], axis=1),
-                jnp.concatenate([real[1], imag[1]], axis=1),
-            ], axis=0))
-            got = dot(high, tables_v[0]) + dot(high, tables_v[1]) + dot(low, tables_v[0])
-            high, low = split(jnp.concatenate([
-                jnp.concatenate([got[0:128, 0:128], got[128:256, 0:128]], axis=1),
-                jnp.concatenate([got[0:128, 128:256], got[128:256, 128:256]], axis=1),
+                jnp.concatenate([got[0][:, 0:128], got[1][:, 0:128]], axis=1),
+                jnp.concatenate([got[0][:, 128:256], got[1][:, 128:256]], axis=1),
             ], axis=0))
             got = dot(tables_v[2], high) + dot(tables_v[3], high) + dot(tables_v[2], low)
             for side in range(2):
@@ -261,7 +261,7 @@
 
             @pl.when(pair == 0)
             def _():
-                back[0] = made[3, 0]
+                keep.start()
 
             out_copy(2 * pair + 1).start()
 
@@ -280,6 +280,8 @@
     def _(j):
         in_copy(j).wait_send()
         out_copy(j).wait()
+
+    keep.wait()
 
     @pl.when(d < n_depth - 1)
     def _():
@@ -289,13 +291,25 @@
             def _(pair):
                 hop_copy(s, pair).wait_send()
 
+
+def finish(listed_s, counts_s, back, out, out_v, sem):
+    u = lax.axis_index("tile")
+    last = lax.axis_size("depth") - 1 - lax.axis_index("depth") + STEPS - 1
+
+    def put(p):
+        return pltpu.make_async_copy(out_v.at[p], out.at[p], sem.at[p])
+
     @pl.loop(0, 8)
     def _(p):
-        last = first + STEPS - 1
         real, imag = decode(back[slot_of(lax.rem(u - listed_s[0, p, last] + 8, 8))])
         live = p < counts_s[0, last]
-        out[p, 0] = jnp.where(live, real, 0.0)
-        out[p, 1] = jnp.where(live, imag, 0.0)
+        out_v[p, 0] = jnp.where(live, real, 0.0)
+        out_v[p, 1] = jnp.where(live, imag, 0.0)
+        put(p).start()
+
+    @pl.loop(0, 8)
+    def _(p):
+        put(p).wait()
 
 
 def per_device(fronts, probe_wave, object_slices, patch_list, counts):
@@ -303,11 +317,13 @@
     batches = counts.shape[0]
     any_space = pl.BlockSpec(memory_space=pl.ANY)
     vmem = pl.BlockSpec(memory_space=pltpu.VMEM)
-    result = pl.pallas_call(
+    listed = jnp.transpose(patch_list[:, 0], (1, 2, 0))
+    counted = jnp.transpose(counts)
+    back = pl.pallas_call(
         kernel,
-        out_shape=jax.ShapeDtypeStruct((8, 2, 128, 128), jnp.float32),
+        out_shape=jax.ShapeDtypeStruct((8, ROWS, 128), jnp.int16),
         in_specs=[any_space] * 6,
-        out_specs=vmem,
+        out_specs=any_space,
         scratch_shapes=[
             pltpu.SMEM((3, 8, batches), jnp.int32),
             pltpu.SMEM((1, batches), jnp.int32),
@@ -324,8 +340,7 @@
             pltpu.VMEM((8, ROWS, 128), jnp.int16),
             pltpu.VMEM((STEPS, 8, ROWS, 128), jnp.int16),
             pltpu.VMEM((STEPS, 8, ROWS, 128), jnp.int16),
-            pltpu.VMEM((8, ROWS, 128), jnp.int16),
-            pltpu.SemaphoreType.DMA((9,)),
+            pltpu.SemaphoreType.DMA((10,)),
             pltpu.SemaphoreType.DMA((8,)),
             pltpu.SemaphoreType.DMA((8,)),
             pltpu.SemaphoreType.DMA((8,)),
@@ -338,9 +353,16 @@
         compiler_params=pltpu.CompilerParams(
             collective_id=0, has_side_effects=True, vmem_limit_bytes=60 * 1024 * 1024
         ),
-    )(
-        jnp.transpose(patch_list[:, 0], (1, 2, 0)), jnp.transpose(counts), fronts[0, 0], probe_wave, object_slices, tables
-    )
+    )(listed, counted, fronts[0, 0], probe_wave, object_slices, tables)
+    smem = pl.BlockSpec(memory_space=pltpu.SMEM)
+    result = pl.pallas_call(
+        finish,
+        out_shape=jax.ShapeDtypeStruct((8, 2, 128, 128), jnp.float32),
+        in_specs=[smem, smem, vmem],
+        out_specs=any_space,
+        scratch_shapes=[pltpu.VMEM((8, 2, 128, 128), jnp.float32), pltpu.SemaphoreType.DMA((8,))],
+        compiler_params=pltpu.CompilerParams(vmem_limit_bytes=60 * 1024 * 1024),
+    )(listed, counted, back)
     return result[None, None]
 
 

time: 53.5 us -> 51.5 us (0.963)
  local copies, waits for them, and re-layouts: 2.3 us -> 0 us
    unnamed x1 -> x0, local copies, waits for them, and re-layouts: 2.3 us -> none
    pallas_call x1 -> x2, Pallas kernels: 51 us -> 51.3 us  [the longest x1 49.1 us: per_device(): pl.pallas_call(kernel, out_shape=jax.ShapeDtypeStruct((8, ROWS, 128), jnp...]
where the time goes in v3:
time: 51.5 us; the launch traced here: 51.3 us
  Pallas kernels  51.3 us (100%)
    pallas_call x1, Pallas kernels, per_device(): pl.pallas_call(kernel, out_shape=jax.ShapeDtypeStruct((8, ROWS, 128), jnp...  49.1 us
    pallas_call x1, Pallas kernels, per_device(): pl.pallas_call(finish, out_shape=jax.ShapeDtypeStruct((8, 2, 128, 128), j...  2.15 us

profile of v3, /device:TPU:6, one launch (start us, length us, event | category | flops | bytes accessed | tf_op | source)
XLA Modules:
  0.0 51.3 jit_solution(14677517241705612441)
XLA Ops:
  0.0 49.1 %shard_map.64.back = s16[8,272,128]{2,1,0:T(8,128)(2,1)} custom-call(s32[3,8,35]{2,1,0:T(8,128)} %bitcast.7, s32[1,35]{1,0:T(1,128)} %bitcast.9, f32[8,2,128,128]{3,2,1,0:T(8,128)} %bitcast.6, f32[2,128,128]{2,1,0:T(8,128)} %probe.1, bf16[2,2,384,384]{3,2,1,0:T(8,128)(2,1)} %obj.1, bf16[4,256,256]{2,1,0:T(8,128)(2,1)} %constant.2.clone.tables), custom_call_target="tpu_custom_call" | custom-call | tf_op jit(solution)/shard_map/pallas_call | solution.py:322
  49.1 2.1 %shard_map.65 = f32[8,2,128,128]{3,2,1,0:T(8,128)} custom-call(s32[3,8,35]{2,1,0:T(8,128)} %bitcast.8, s32[1,35]{1,0:T(1,128)} %bitcast.10, s16[8,272,128]{2,1,0:T(8,128)(2,1)} %shard_map.64.back), custom_call_target="tpu_custom_call" | custom-call | tf_op jit(solution)/shard_map/pallas_call | solution.py:358

commit v4 on v3

--- a/solution.py
+++ b/solution.py
@@ -242,10 +242,13 @@
                 jnp.concatenate([got[0][:, 0:128], got[1][:, 0:128]], axis=1),
                 jnp.concatenate([got[0][:, 128:256], got[1][:, 128:256]], axis=1),
             ], axis=0))
-            got = dot(tables_v[2], high) + dot(tables_v[3], high) + dot(tables_v[2], low)
+            got = [
+                dot(tables_v[2, rows], high) + dot(tables_v[3, rows], high) + dot(tables_v[2, rows], low)
+                for rows in (pl.ds(0, 128), pl.ds(128, 128))
+            ]
             for side in range(2):
-                real[side] = got[0:128, side * 128:(side + 1) * 128]
-                imag[side] = got[128:256, side * 128:(side + 1) * 128]
+                real[side] = got[0][:, side * 128:(side + 1) * 128]
+                imag[side] = got[1][:, side * 128:(side + 1) * 128]
         for side in range(2):
             store_wave(made.at[s, 2 * pair + side], real[side], imag[side])
 

time: 51.5 us -> 50.5 us (0.981)
  Pallas kernels: 51.3 us -> 50.2 us
    pallas_call x1, Pallas kernels: 49.1 us -> 48.1 us  [per_device(): pl.pallas_call(kernel, out_shape=jax.ShapeDtypeStruct((8, ROWS, 128), jnp...]
where the time goes in v4:
time: 50.5 us; the launch traced here: 50.2 us
  Pallas kernels  50.2 us (99%)
    pallas_call x1, Pallas kernels, per_device(): pl.pallas_call(kernel, out_shape=jax.ShapeDtypeStruct((8, ROWS, 128), jnp...  48.1 us
    pallas_call x1, Pallas kernels, per_device(): pl.pallas_call(finish, out_shape=jax.ShapeDtypeStruct((8, 2, 128, 128), j...  2.15 us

profile of v4, /device:TPU:6, one launch (start us, length us, event | category | flops | bytes accessed | tf_op | source)
XLA Modules:
  0.0 50.2 jit_solution(2289785700892933769)
XLA Ops:
  0.0 48.1 %shard_map.64.back = s16[8,272,128]{2,1,0:T(8,128)(2,1)} custom-call(s32[3,8,35]{2,1,0:T(8,128)} %bitcast.7, s32[1,35]{1,0:T(1,128)} %bitcast.9, f32[8,2,128,128]{3,2,1,0:T(8,128)} %bitcast.6, f32[2,128,128]{2,1,0:T(8,128)} %probe.1, bf16[2,2,384,384]{3,2,1,0:T(8,128)(2,1)} %obj.1, bf16[4,256,256]{2,1,0:T(8,128)(2,1)} %constant.2.clone.tables), custom_call_target="tpu_custom_call" | custom-call | tf_op jit(solution)/shard_map/pallas_call | solution.py:325
  48.1 2.1 %shard_map.65 = f32[8,2,128,128]{3,2,1,0:T(8,128)} custom-call(s32[3,8,35]{2,1,0:T(8,128)} %bitcast.8, s32[1,35]{1,0:T(1,128)} %bitcast.10, s16[8,272,128]{2,1,0:T(8,128)(2,1)} %shard_map.64.back), custom_call_target="tpu_custom_call" | custom-call | tf_op jit(solution)/shard_map/pallas_call | solution.py:361

commit v5 on v4

--- a/solution.py
+++ b/solution.py
@@ -237,15 +237,19 @@
             got = []
             for side in range(2):
                 high, low = split(jnp.concatenate([real[side], imag[side]], axis=1))
-                got.append(dot(high, tables_v[0]) + dot(high, tables_v[1]) + dot(low, tables_v[0]))
+                got.append(jnp.concatenate([
+                    dot(high[i:i + 64], tables_v[0]) + dot(high[i:i + 64], tables_v[1]) + dot(low[i:i + 64], tables_v[0])
+                    for i in (0, 64)
+                ], axis=0))
             high, low = split(jnp.concatenate([
                 jnp.concatenate([got[0][:, 0:128], got[1][:, 0:128]], axis=1),
                 jnp.concatenate([got[0][:, 128:256], got[1][:, 128:256]], axis=1),
             ], axis=0))
             got = [
                 dot(tables_v[2, rows], high) + dot(tables_v[3, rows], high) + dot(tables_v[2, rows], low)
-                for rows in (pl.ds(0, 128), pl.ds(128, 128))
+                for rows in (pl.ds(0, 64), pl.ds(64, 64), pl.ds(128, 64), pl.ds(192, 64))
             ]
+            got = [jnp.concatenate(got[0:2], axis=0), jnp.concatenate(got[2:4], axis=0)]
             for side in range(2):
                 real[side] = got[0][:, side * 128:(side + 1) * 128]
                 imag[side] = got[1][:, side * 128:(side + 1) * 128]
@@ -304,7 +308,7 @@
 
     @pl.loop(0, 8)
     def _(p):
-        real, imag = decode(back[slot_of(lax.rem(u - listed_s[0, p, last] + 8, 8))])
+        real, imag = decode(back[slot_of(lax.bitwise_and(u - listed_s[0, p, last], 7))])
         live = p < counts_s[0, last]
         out_v[p, 0] = jnp.where(live, real, 0.0)
         out_v[p, 1] = jnp.where(live, imag, 0.0)

time: 50.5 us -> 54.2 us (1.073)
  Pallas kernels: 50.2 us -> 53.9 us
    pallas_call x1, Pallas kernels: 48.1 us -> 51.8 us  [per_device(): pl.pallas_call(kernel, out_shape=jax.ShapeDtypeStruct((8, ROWS, 128), jnp...]
where the time goes in v5:
time: 54.2 us; the launch traced here: 53.9 us
  Pallas kernels  53.9 us (99%)
    pallas_call x1, Pallas kernels, per_device(): pl.pallas_call(kernel, out_shape=jax.ShapeDtypeStruct((8, ROWS, 128), jnp...  51.8 us
    pallas_call x1, Pallas kernels, per_device(): pl.pallas_call(finish, out_shape=jax.ShapeDtypeStruct((8, 2, 128, 128), j...  2.14 us

profile of v5, /device:TPU:6, one launch (start us, length us, event | category | flops | bytes accessed | tf_op | source)
XLA Modules:
  0.0 53.9 jit_solution(4689896464875735263)
XLA Ops:
  0.0 51.8 %shard_map.64.back = s16[8,272,128]{2,1,0:T(8,128)(2,1)} custom-call(s32[3,8,35]{2,1,0:T(8,128)} %bitcast.7, s32[1,35]{1,0:T(1,128)} %bitcast.9, f32[8,2,128,128]{3,2,1,0:T(8,128)} %bitcast.6, f32[2,128,128]{2,1,0:T(8,128)} %probe.1, bf16[2,2,384,384]{3,2,1,0:T(8,128)(2,1)} %obj.1, bf16[4,256,256]{2,1,0:T(8,128)(2,1)} %constant.2.clone.tables), custom_call_target="tpu_custom_call" | custom-call | tf_op jit(solution)/shard_map/pallas_call | solution.py:329
  51.8 2.1 %shard_map.65 = f32[8,2,128,128]{3,2,1,0:T(8,128)} custom-call(s32[3,8,35]{2,1,0:T(8,128)} %bitcast.8, s32[1,35]{1,0:T(1,128)} %bitcast.10, s16[8,272,128]{2,1,0:T(8,128)(2,1)} %shard_map.64.back), custom_call_target="tpu_custom_call" | custom-call | tf_op jit(solution)/shard_map/pallas_call | solution.py:365

commit v6 on v4

--- a/solution.py
+++ b/solution.py
@@ -304,7 +304,7 @@
 
     @pl.loop(0, 8)
     def _(p):
-        real, imag = decode(back[slot_of(lax.rem(u - listed_s[0, p, last] + 8, 8))])
+        real, imag = decode(back[slot_of(lax.bitwise_and(u - listed_s[0, p, last], 7))])
         live = p < counts_s[0, last]
         out_v[p, 0] = jnp.where(live, real, 0.0)
         out_v[p, 1] = jnp.where(live, imag, 0.0)

time: 50.5 us -> 50.5 us (level)
  no operation moved by 1% of the time
where the time goes in v6:
time: 50.5 us; the launch traced here: 50.2 us
  Pallas kernels  50.2 us (99%)
    pallas_call x1, Pallas kernels, per_device(): pl.pallas_call(kernel, out_shape=jax.ShapeDtypeStruct((8, ROWS, 128), jnp...  48.1 us
    pallas_call x1, Pallas kernels, per_device(): pl.pallas_call(finish, out_shape=jax.ShapeDtypeStruct((8, 2, 128, 128), j...  2.14 us

profile of v6, /device:TPU:6, one launch (start us, length us, event | category | flops | bytes accessed | tf_op | source)
XLA Modules:
  0.0 50.2 jit_solution(925652392131320453)
XLA Ops:
  0.0 48.1 %shard_map.64.back = s16[8,272,128]{2,1,0:T(8,128)(2,1)} custom-call(s32[3,8,35]{2,1,0:T(8,128)} %bitcast.7, s32[1,35]{1,0:T(1,128)} %bitcast.9, f32[8,2,128,128]{3,2,1,0:T(8,128)} %bitcast.6, f32[2,128,128]{2,1,0:T(8,128)} %probe.1, bf16[2,2,384,384]{3,2,1,0:T(8,128)(2,1)} %obj.1, bf16[4,256,256]{2,1,0:T(8,128)(2,1)} %constant.2.clone.tables), custom_call_target="tpu_custom_call" | custom-call | tf_op jit(solution)/shard_map/pallas_call | solution.py:325
  48.1 2.1 %shard_map.65 = f32[8,2,128,128]{3,2,1,0:T(8,128)} custom-call(s32[3,8,35]{2,1,0:T(8,128)} %bitcast.8, s32[1,35]{1,0:T(1,128)} %bitcast.10, s16[8,272,128]{2,1,0:T(8,128)(2,1)} %shard_map.64.back), custom_call_target="tpu_custom_call" | custom-call | tf_op jit(solution)/shard_map/pallas_call | solution.py:361
